TPU v7x, 32 devices: a whole 2x2x4 slice. The times are simulated.
32 devices in a mesh: grp: 2 (over x), ex: 4 (over y, core), at: 4 (over z).
Axes of the slice: x: 2, y: 2, z: 4, core: 2. Of those that a mesh axis runs over, the one named last changes fastest.
Arguments:
- tokens: bfloat16 [256, 7168], P(('grp', 'ex', 'at')), parts along dimension 0, may hold values from -6 to 6
- expert_ids: int32 [256, 8], P(('grp', 'ex', 'at')), parts along dimension 0, may hold values from 0 to 15, all different within a row; in each aligned block of 8 rows (0 to 7, 8 to 15, ...) at most 5 rows name the same one
- gates: bfloat16 [256, 8], P(('grp', 'ex', 'at')), parts along dimension 0, may hold values from 0.099609375 to 0.59765625
- w_in: bfloat16 [16, 7168, 2, 2048], P('ex', None, None, 'at'), may hold values from -0.0625 to 0.0625
- w_out: bfloat16 [16, 2048, 7168], P('ex', 'at'), may hold values from -0.125 to 0.125
- q_latent: bfloat16 [128, 64, 512], P(('grp', 'ex', 'at')), parts along dimension 0, may hold values from -8 to 8
- q_rope: bfloat16 [128, 4096], P(('grp', 'ex', 'at')), parts along dimension 0, may hold values from -8 to 8
- cache_latent: bfloat16 [128, 256, 512], P(('grp', 'ex', 'at')), parts along dimension 0, may hold values from -4 to 4
- cache_rope: bfloat16 [128, 64, 256], P(('grp', 'ex', 'at')), parts along dimension 0, may hold values from -4 to 4
- lengths: int32 [128], P(('grp', 'ex', 'at')), parts along dimension 0, may hold values from 2 to 256, as said below
Outputs:
- moe_out: bfloat16 [256, 7168], P(('grp', 'ex', 'at')), parts along dimension 0
- context: bfloat16 [128, 64, 512], P(('grp', 'ex', 'at')), parts along dimension 0
There are 2 independent parts, one for each index of `grp`. A program takes and returns all parts, laid end to end along the dimension named above; an argument that names none is the same for every part. Nothing has to cross between parts.
Inputs may be any that keep to these rules, and one draw needn't show every extreme that they name: `expert_ids`: A row's 8 ids differ. In each aligned block of 8 rows (the rows of one device) no expert is named by more than 5 rows, and in every draw some block has an expert named by exactly 5 rows. `lengths`: in each aligned block of 4 sequences (those of one device) one sequence has 256 positions.
All inputs are finite; a program needn't handle non-finite values.
Results may differ from a plain program's by a relative error of at most 0.0085.
Values may be sent and summed in bfloat16 or wider, within the bound.
A program may use at most 320 MiB of HBM per device.

v0:
```python
import jax
import jax.numpy as jnp
from jax import lax
from jax.sharding import PartitionSpec as P

CAP = 5


def expert_part(row_block, row_gates, w_in, w_out):
    slot_count, model_width, pair_count, hid_units = w_in.shape
    gate_up = jnp.einsum(
        "srd,sdf->srf",
        row_block,
        w_in.reshape(slot_count, model_width, pair_count * hid_units),
        preferred_element_type=jnp.float32,
    )
    hidden = (jax.nn.silu(gate_up[..., :hid_units]) * gate_up[..., hid_units:]).astype(jnp.bfloat16)
    down_out = jnp.einsum("srf,sfd->srd", hidden, w_out, preferred_element_type=jnp.float32)
    return (down_out * row_gates[..., None].astype(jnp.float32)).astype(jnp.bfloat16)


def latent_attention(q_latent, q_rope, cache_latent, cache_rope, lengths):
    att_rows, head_count, latent_width = q_latent.shape
    positions = cache_latent.shape[1]
    rope_q = q_rope.reshape(att_rows, head_count, -1)
    scores = jnp.einsum("ahl,acl->ahc", q_latent, cache_latent, preferred_element_type=jnp.float32)
    scores = scores + jnp.einsum(
        "ahr,arc->ahc", rope_q, cache_rope, preferred_element_type=jnp.float32
    )
    scores = scores * 192.0 ** (-0.5)
    visible = jnp.arange(positions)[None, None, :] < lengths[:, None, None]
    scores = jnp.where(visible, scores, -1e30)
    peak = jnp.max(scores, axis=2, keepdims=True)
    expo = jnp.where(visible, jnp.exp(scores - peak), 0.0)
    probs = (expo / jnp.sum(expo, axis=2, keepdims=True)).astype(jnp.bfloat16)
    context = jnp.einsum("ahc,acl->ahl", probs, cache_latent, preferred_element_type=jnp.float32)
    return context.astype(jnp.bfloat16)


def per_device(
    tokens, expert_ids, gates, w_in, w_out, q_latent, q_rope, cache_latent, cache_rope, lengths
):
    tok_rows, model_width = tokens.shape
    top_count = expert_ids.shape[1]
    slot_count = w_in.shape[0]
    ex_count = lax.axis_size("ex")
    at_count = lax.axis_size("at")
    experts = slot_count * ex_count
    slot_rows = experts * CAP
    flat_ids = expert_ids.reshape(-1)
    onehot = (flat_ids[:, None] == jnp.arange(experts)[None, :]).astype(jnp.int32)
    before = jnp.cumsum(onehot, axis=0) - onehot
    position = jnp.sum(before * onehot, axis=1)
    column = flat_ids // slot_count
    slot_index = flat_ids % slot_count
    target = (slot_index * ex_count + column) * CAP + position
    placed = target[None, :] == jnp.arange(slot_rows)[:, None]
    placed_rows = placed.reshape(slot_rows, tok_rows, top_count).any(axis=2).astype(jnp.bfloat16)
    packed = jnp.dot(placed_rows, tokens, preferred_element_type=jnp.float32).astype(jnp.bfloat16)
    packed = packed.reshape(slot_count, ex_count, CAP, model_width)
    packed_gates = jnp.dot(
        placed.astype(jnp.bfloat16), gates.reshape(-1), preferred_element_type=jnp.float32
    )
    packed_gates = packed_gates.astype(jnp.bfloat16).reshape(slot_count, ex_count, CAP)
    spread = jnp.broadcast_to(
        packed[:, :, None], (slot_count, ex_count, at_count, CAP, model_width)
    )
    spread = spread.reshape(slot_count, ex_count * at_count, CAP, model_width)
    spread_gates = jnp.broadcast_to(packed_gates[:, :, None], (slot_count, ex_count, at_count, CAP))
    spread_gates = spread_gates.reshape(slot_count, ex_count * at_count, CAP)
    arrived, arrived_gates = (
        lax.all_to_all(spread, ("ex", "at"), split_axis=1, concat_axis=1, tiled=True),
        lax.all_to_all(spread_gates, ("ex", "at"), split_axis=1, concat_axis=1, tiled=True),
    )
    partial_value = expert_part(
        arrived.reshape(slot_count, -1, model_width),
        arrived_gates.reshape(slot_count, -1),
        w_in,
        w_out,
    )
    partial_value = partial_value.reshape(slot_count, ex_count * at_count, CAP, model_width)
    returned = lax.all_to_all(partial_value, ("ex", "at"), split_axis=1, concat_axis=1, tiled=True)
    out_rows = jnp.sum(
        returned.reshape(slot_count, ex_count, at_count, CAP, model_width).astype(jnp.float32),
        axis=2,
    )
    flat_out = out_rows.reshape(slot_rows, model_width)
    moe_out = jnp.sum(flat_out[target.reshape(tok_rows, top_count)], axis=1).astype(jnp.bfloat16)
    context = latent_attention(q_latent, q_rope, cache_latent, cache_rope, lengths)
    return (moe_out, context)


def solution(mesh):
    return jax.shard_map(
        per_device,
        mesh=mesh,
        in_specs=(
            P(("grp", "ex", "at"), None),
            P(("grp", "ex", "at"), None),
            P(("grp", "ex", "at"), None),
            P("ex", None, None, "at"),
            P("ex", "at", None),
            P(("grp", "ex", "at"), None, None),
            P(("grp", "ex", "at"), None),
            P(("grp", "ex", "at"), None, None),
            P(("grp", "ex", "at"), None, None),
            P(("grp", "ex", "at")),
        ),
        out_specs=(P(("grp", "ex", "at"), None), P(("grp", "ex", "at"), None, None)),
        check_vma=False,
    )
```

profile of v0, /device:TPU:0, one launch (start us, length us, event | category | flops | bytes accessed | tf_op | source)
XLA Modules:
  0.0 301.3 jit_solution(3265156133076653071)
XLA Ops:
  0.6 0.9 eq.37
  1.7 0.2 select_reduce_fusion
  1.9 0.8 reshape.153
  2.6 0.1 fusion.9
  2.8 0.1 broadcast_in_dim.44
  2.9 0.6 broadcast_in_dim.45
  3.5 7.4 %all-to-all-start.1 = ((bf16[4,16,5]{2,0,1:T(4,128)(2,1)}), bf16[4,16,5]{2,0,1:T(4,128)(2,1)S(1)}, u32[]{:S(2)}, u32[]{:S(2)}) async-start(bf16[4,16,5]{2,0,1:T(4,128)(2,1)} %bitcast.3), calls=%async_computation.1 | async-start | bytes 32768 | tf_op jit(solution)/shard_map/all_to_all | solution.py:73
  11.0 0.7 compare_select_fusion
  11.8 2.4 convolution_convert_fusion
  14.2 1.6 broadcast_in_dim.42
  15.8 2.0 copy.27
  17.8 4.7 %broadcast_in_dim.43 = bf16[4,4,4,5,7168]{4,0,3,2,1:T(4,128)(2,1)} broadcast(bf16[4,4,5,7168]{3,0,2,1:T(4,128)(2,1)} %copy.27), dimensions={0,1,3,4} | broadcast | bytes 5734400 | tf_op jit(solution)/shard_map/broadcast_in_dim | solution.py:65
  22.6 6.1 %all-to-all-start = ((bf16[4,16,5,7168]{3,0,2,1:T(4,128)(2,1)}), bf16[4,16,5,7168]{3,0,2,1:T(4,128)(2,1)}, u32[]{:S(2)}, u32[]{:S(2)}) async-start(bf16[4,16,5,7168]{3,0,2,1:T(4,128)(2,1)} %bitcast.26), calls=%async_computation | async-start | bytes 9175040 | tf_op jit(solution)/shard_map/all_to_all | solution.py:72
  28.6 92.8 %reshape.135 = bf16[4,7168,1024]{2,1,0:T(8,128)(2,1)} reshape(bf16[4,7168,2,512]{3,2,1,0:T(2,128)(2,1)} %param.13) | data formatting | bytes 117440512 | tf_op jit(solution)/shard_map/reshape | solution.py:14
  121.5 0.1 copy.30
  121.6 0.1 copy.31
  121.8 9.7 %all-to-all-done = bf16[4,16,5,7168]{3,0,2,1:T(4,128)(2,1)} async-done(((bf16[4,16,5,7168]{3,0,2,1:T(4,128)(2,1)}), bf16[4,16,5,7168]{3,0,2,1:T(4,128)(2,1)}, u32[]{:S(2)}, u32[]{:S(2)}) %all-to-all-start) | async-done | bytes 4587552 | tf_op jit(solution)/shard_map/all_to_all | solution.py:72
  131.5 22.2 %fusion.2 = f32[4,80,1024]{2,1,0:T(8,128)S(1)} fusion(bf16[4,7168,1024]{2,1,0:T(8,128)(2,1)} %reshape.135, bf16[4,80,7168]{2,0,1:T(4,128)(2,1)} %bitcast.1), kind=kOutput, calls=%fused_computation.6 | convolution fusion | flops 4697620480 | bytes 64618496 | tf_op jit(solution)/shard_map/srd,sdf->srf/dot_general | solution.py:11
  153.7 16.7 %fusion.1 = bf16[4,80,7168]{2,1,0:T(8,128)(2,1)} fusion(bf16[4,512,7168]{2,1,0:T(8,128)(2,1)} %param.14, f32[4,80]{1,0:T(4,128)S(1)} %reshape.141, f32[4,80,1024]{2,1,0:T(8,128)S(1)} %fusion.2), kind=kOutput, calls=%fused_computation.3 | convolution fusion | flops 2354380800 | bytes 35259648 | tf_op jit(solution)/shard_map/srf,sfd->srd/dot_general | solution.py:18
  170.3 7.9 %copy.32 = bf16[4,80,7168]{2,0,1:T(4,128)(2,1)} copy(bf16[4,80,7168]{2,1,0:T(8,128)(2,1)} %fusion.1) | data formatting | bytes 9175040 | tf_op jit(solution)/shard_map/convert_element_type | solution.py:19
  178.2 4.9 %all-to-all-start.2 = ((bf16[4,16,5,7168]{3,0,2,1:T(4,128)(2,1)}), bf16[4,16,5,7168]{3,0,2,1:T(4,128)(2,1)}, u32[]{:S(2)}, u32[]{:S(2)}) async-start(bf16[4,16,5,7168]{3,0,2,1:T(4,128)(2,1)} %bitcast.25), calls=%async_computation.2 | async-start | bytes 9175040 | tf_op jit(solution)/shard_map/all_to_all | solution.py:82
  183.3 0.1 reshape.140
  183.5 0.4 fusion.32
  183.9 0.2 fusion.6
  184.1 0.2 fusion.31
  184.3 1.3 convolution_convert_fusion.1
  185.6 100.2 %all-to-all-done.2 = bf16[4,16,5,7168]{3,0,2,1:T(4,128)(2,1)} async-done(((bf16[4,16,5,7168]{3,0,2,1:T(4,128)(2,1)}), bf16[4,16,5,7168]{3,0,2,1:T(4,128)(2,1)}, u32[]{:S(2)}, u32[]{:S(2)}) %all-to-all-start.2) | async-done | bytes 4587552 | tf_op jit(solution)/shard_map/all_to_all | solution.py:82
  285.8 5.1 %convert_reduce_fusion = f32[4,4,5,7168]{3,0,2,1:T(4,128)S(1)} fusion(bf16[4,16,5,7168]{3,0,2,1:T(4,128)(2,1)} %all-to-all-done.2), kind=kLoop, calls=%fused_computation.4 | loop fusion | flops 4014080 | bytes 6881280 | tf_op jit(solution)/shard_map/reduce_sum | solution.py:83
  290.8 3.2 %copy.33 = f32[4,4,5,7168]{3,2,1,0:T(8,128)} copy(f32[4,4,5,7168]{3,0,2,1:T(4,128)S(1)} %convert_reduce_fusion) | data formatting | bytes 4587520 | tf_op jit(solution)/shard_map/reduce_sum | solution.py:83
  294.0 2.3 reshape.139
  296.3 2.3 gather_fusion
  298.7 2.6 bitcast_reduce_fusion
  (21 shorter events, 0.6 us)
Async XLA Ops:
  0.6 182.9 %copy-start = (bf16[4,256,512]{2,1,0:T(8,128)(2,1)S(1)}, bf16[4,256,512]{2,1,0:T(8,128)(2,1)}, u32[]{:S(2)}) copy-start(bf16[4,256,512]{2,1,0:T(8,128)(2,1)} %param.17) | copy-start | bytes 3145732
  3.5 14.3 %all-to-all-start.1 = ((bf16[4,16,5]{2,0,1:T(4,128)(2,1)}), bf16[4,16,5]{2,0,1:T(4,128)(2,1)S(1)}, u32[]{:S(2)}, u32[]{:S(2)}) async-start(bf16[4,16,5]{2,0,1:T(4,128)(2,1)} %bitcast.3), calls=%async_computation.1 | async-start | bytes 32768 | tf_op jit(solution)/shard_map/all_to_all | solution.py:73
  22.6 108.9 %all-to-all-start = ((bf16[4,16,5,7168]{3,0,2,1:T(4,128)(2,1)}), bf16[4,16,5,7168]{3,0,2,1:T(4,128)(2,1)}, u32[]{:S(2)}, u32[]{:S(2)}) async-start(bf16[4,16,5,7168]{3,0,2,1:T(4,128)(2,1)} %bitcast.26), calls=%async_computation | async-start | bytes 9175040 | tf_op jit(solution)/shard_map/all_to_all | solution.py:72
  178.2 5.0 %copy-start.3 = (bf16[4,4096]{1,0:T(4,128)(2,1)S(1)}, bf16[4,4096]{1,0:T(4,128)(2,1)}, u32[]{:S(2)}) copy-start(bf16[4,4096]{1,0:T(4,128)(2,1)} %param.16) | copy-start | bytes 98308
  178.2 5.2 %copy-start.4 = (s32[4]{0:T(128)S(1)}, s32[4]{0:T(128)}, u32[]{:S(2)}) copy-start(s32[4]{0:T(128)} %param.19) | copy-start | bytes 52
  178.2 5.3 %copy-start.1 = (bf16[4,64,512]{2,1,0:T(8,128)(2,1)S(1)}, bf16[4,64,512]{2,1,0:T(8,128)(2,1)}, u32[]{:S(2)}) copy-start(bf16[4,64,512]{2,1,0:T(8,128)(2,1)} %param.15) | copy-start | bytes 786436
  178.2 5.7 %copy-start.2 = (bf16[4,64,256]{2,1,0:T(8,128)(2,1)S(1)}, bf16[4,64,256]{2,1,0:T(8,128)(2,1)}, u32[]{:S(2)}) copy-start(bf16[4,64,256]{2,1,0:T(8,128)(2,1)} %param.18) | copy-start | bytes 393220
  178.2 107.5 %all-to-all-start.2 = ((bf16[4,16,5,7168]{3,0,2,1:T(4,128)(2,1)}), bf16[4,16,5,7168]{3,0,2,1:T(4,128)(2,1)}, u32[]{:S(2)}, u32[]{:S(2)}) async-start(bf16[4,16,5,7168]{3,0,2,1:T(4,128)(2,1)} %bitcast.25), calls=%async_computation.2 | async-start | bytes 9175040 | tf_op jit(solution)/shard_map/all_to_all | solution.py:82
where the time goes:
time: 304 us; the launch traced here: 301 us
  local copies, waits for them, and re-layouts  120 us (39%)
  waiting for transfers between devices  110 us (36%)
  matrix products  43.3 us (14%)
  starting transfers between devices  18.4 us (6%)
  other arithmetic  9.11 us (3%)
    all_to_all x1, waiting for transfers between devices, per_device(): lax.all_to_all(partial_value, ('ex', 'at'), split_axis=1, concat_axis=1,...  100 us
    reshape x1, local copies, waits for them, and re-layouts, expert_part(): w_in.reshape(slot_count, model_width, pair_count * hid_units)  92.8 us
    dot_general x1, matrix products, expert_part(): jnp.einsum('srd,sdf->srf', row_block, w_in.reshape(slot_count, model_widt...  22.2 us
    dot_general x1, matrix products, expert_part(): jnp.einsum('srf,sfd->srd', hidden, w_out, preferred_element_type=jnp.floa...  16.7 us
    all_to_all x1, waiting for transfers between devices, per_device(): lax.all_to_all(spread, ('ex', 'at'), split_axis=1, concat_axis=1, tiled=T...  9.7 us
    broadcast_in_dim x3, local copies, waits for them, and re-layouts, per_device(): jnp.broadcast_to(packed[:, :, None], (slot_count, ex_count, at_count, CAP...  8.34 us
    convert_element_type x1, local copies, waits for them, and re-layouts, expert_part(): (down_out * row_gates[..., None].astype(jnp.float32)).astype(jnp.bfloat16)  7.89 us
    all_to_all x1, starting transfers between devices, per_device(): lax.all_to_all(spread_gates, ('ex', 'at'), split_axis=1, concat_axis=1, t...  7.39 us
  transfers between devices with their start and end apart: 3, of which 2 were waited for; matrix products, arithmetic and copies ran while one was open for 34% of the time, Pallas kernels for 0%

commit v1 on v0

--- a/solution.py
+++ b/solution.py
@@ -1,9 +1,269 @@
+import functools
+
 import jax
 import jax.numpy as jnp
 from jax import lax
+from jax.experimental import pallas as pl
+from jax.experimental.pallas import tpu as pltpu
 from jax.sharding import PartitionSpec as P
 
 CAP = 5
+LANES = 128
+D_BLOCK = 1024
+W_SLOTS = 12
+O_COLS = 512
+O_SLOTS = 6
+
+
+def moe_kernel(
+    x_ref, win_ref, wout_ref, o_ref,
+    xg, xe, wbuf, obuf, acc, hid, keep1, out1, in1, keep2, out2, in2, keep3, out3, in3,
+    wsem, osem, zs, zr, ys, yr, cs, cr, s1, q1, s2, q2, s3, q3,
+):
+    experts_here, model_width, jbs = win_ref.shape[:3]
+    hid_units = wout_ref.shape[1]
+    at_count = 4
+    tok_rows = x_ref.shape[0]
+    rows = 16 * tok_rows
+    e0 = lax.axis_index("ex")
+    a0 = lax.axis_index("at")
+    y0 = e0 // 2
+    c0 = e0 % 2
+    e_y = (1 - y0) * 2 + c0
+    e_c = y0 * 2 + (1 - c0)
+    d_chunks = model_width // D_BLOCK
+    w_chunks = experts_here * d_chunks
+    o_chunks = model_width // O_COLS
+
+    def w_copy(i, jb):
+        return pltpu.make_async_copy(
+            win_ref.at[i // d_chunks, pl.ds((i % d_chunks) * D_BLOCK, D_BLOCK), jb],
+            wbuf.at[i % W_SLOTS, jb],
+            wsem.at[i % W_SLOTS, jb],
+        )
+
+    def o_copy(i):
+        return pltpu.make_async_copy(
+            wout_ref.at[:, :, pl.ds(pl.multiple_of(i * O_COLS, O_COLS), O_COLS)],
+            obuf.at[i % O_SLOTS],
+            osem.at[i % O_SLOTS],
+        )
+
+    def w_start(i, carry):
+        for jb in range(jbs):
+            w_copy(i, jb).start()
+        return carry
+
+    def o_start(i, carry):
+        o_copy(i).start()
+        return carry
+
+    lax.fori_loop(0, W_SLOTS, w_start, 0)
+
+    to_z = [{"ex": e0, "at": (a0 + j) % at_count} for j in range(at_count)]
+    to_y = {"ex": e_y, "at": a0}
+    to_c = {"ex": e_c, "at": a0}
+    barrier = pltpu.get_barrier_semaphore()
+    for peer in to_z[1:] + [to_y, to_c]:
+        pl.semaphore_signal(barrier, inc=1, device_id=peer, device_id_type=pl.DeviceIdType.MESH)
+    pl.semaphore_wait(barrier, at_count + 1)
+
+    def remote(src, dst, send, recv, peer):
+        return pltpu.make_async_remote_copy(
+            src_ref=src, dst_ref=dst, send_sem=send, recv_sem=recv,
+            device_id=peer, device_id_type=pl.DeviceIdType.MESH,
+        )
+
+    def block(ex, j):
+        return ex * at_count + (a0 + at_count - j) % at_count
+
+    def z_copy(j, slot):
+        return remote(xg.at[slot], xg.at[slot], zs.at[j - 1], zr.at[j - 1], to_z[j])
+
+    def y_copy(j, slot):
+        return remote(xg.at[slot], xg.at[slot], ys.at[j], yr.at[j], to_y)
+
+    def c_copy(j, slot):
+        return remote(xg.at[slot], xg.at[slot], cs.at[j], cr.at[j], to_c)
+
+    own = block(e0, 0)
+    xg[own] = x_ref[...]
+    for j in range(1, at_count):
+        z_copy(j, own).start()
+    y_copy(0, own).start()
+    c_copy(0, own).start()
+    lax.fori_loop(0, O_SLOTS, o_start, 0)
+    for j in (1, 3, 2):
+        z_copy(j, block(e0, j)).wait_recv()
+        y_copy(j, block(e0, j)).start()
+        c_copy(j, block(e0, j)).start()
+    for j in (0, 1, 3, 2):
+        y_copy(j, block(e_y, j)).wait_recv()
+        c_copy(4 + j, block(e_y, j)).start()
+    for j in (0, 1, 3, 2):
+        c_copy(j, block(e_c, j)).wait_recv()
+    for j in (0, 1, 3, 2):
+        c_copy(4 + j, block((1 - y0) * 2 + (1 - c0), j)).wait_recv()
+
+    row = lax.broadcasted_iota(jnp.int32, (LANES, 2 * LANES), 0)
+    col = lax.broadcasted_iota(jnp.int32, (LANES, 2 * LANES), 1)
+    spread = [(col == 2 * row + p).astype(jnp.bfloat16) for p in range(2)]
+
+    def expand(i, carry):
+        x = xg[:, :, pl.ds(pl.multiple_of(i * LANES, LANES), LANES)].astype(jnp.float32)
+        x = x.reshape(rows, LANES).astype(jnp.bfloat16)
+        for p in range(2):
+            xe[p * rows:(p + 1) * rows, pl.ds(pl.multiple_of(i * 2 * LANES, 2 * LANES), 2 * LANES)] = (
+                jnp.dot(x, spread[p], preferred_element_type=jnp.float32).astype(jnp.bfloat16)
+            )
+        return carry
+
+    lax.fori_loop(0, model_width // LANES, expand, 0)
+    dense = xg[:, :, model_width:model_width + LANES].astype(jnp.float32).reshape(rows, LANES)
+    lane = lax.broadcasted_iota(jnp.int32, (rows, LANES), 1)
+
+    def one_expert(e, carry):
+        acc[...] = jnp.zeros_like(acc)
+
+        def step(d, inner):
+            i = e * d_chunks + d
+            for jb in range(jbs):
+                w_copy(i, jb).wait()
+            view = wbuf.at[i % W_SLOTS].reshape(jbs, 2 * D_BLOCK, LANES)
+            x = xe[:, pl.ds(pl.multiple_of(d * 2 * D_BLOCK, 2 * D_BLOCK), 2 * D_BLOCK)]
+            w = jnp.concatenate([view[jb] for jb in range(jbs)], axis=1)
+            acc[...] += jnp.dot(x, w, preferred_element_type=jnp.float32)
+
+            @pl.when(i + W_SLOTS < w_chunks)
+            def _():
+                w_start(i + W_SLOTS, 0)
+
+            return inner
+
+        lax.fori_loop(0, d_chunks, step, 0)
+        gate = jnp.sum(jnp.where(lane == e0 * experts_here + e, dense, 0.0), axis=1, keepdims=True)
+        hidden = jax.nn.silu(acc[:rows, :]) * acc[rows:, :] * gate
+        hid[:, pl.ds(pl.multiple_of(e * hid_units, hid_units), hid_units)] = hidden.astype(jnp.bfloat16)
+        return carry
+
+    lax.fori_loop(0, experts_here, one_expert, 0)
+
+    def core_copy(i):
+        return remote(out1.at[i], in1.at[i], s1.at[i], q1.at[i], to_c)
+
+    def row_copy(i):
+        return remote(out2.at[i], in2.at[i], s2.at[i], q2.at[i], to_y)
+
+    def col_copy(i, j):
+        return remote(
+            out3.at[i, (a0 + j) % at_count], in3.at[i, j - 1], s3.at[i, j - 1], q3.at[i, j - 1], to_z[j]
+        )
+
+    def down(i, carry):
+        @pl.when(i < o_chunks)
+        def _():
+            o_copy(i).wait()
+            w = obuf[i % O_SLOTS].reshape(experts_here * hid_units, O_COLS)
+            part = jnp.dot(hid[...], w, preferred_element_type=jnp.float32)
+            part = part.reshape(2, 2, rows // 4, O_COLS)
+            keep1[i] = jnp.where(c0 == 0, part[:, 0], part[:, 1])
+            out1[i] = jnp.where(c0 == 0, part[:, 1], part[:, 0]).astype(jnp.bfloat16)
+            core_copy(i).start()
+
+            @pl.when(i + O_SLOTS < o_chunks)
+            def _():
+                o_start(i + O_SLOTS, 0)
+
+        @pl.when((i >= 1) & (i < o_chunks + 1))
+        def _():
+            k = i - 1
+            core_copy(k).wait_recv()
+            total = keep1[k] + in1[k].astype(jnp.float32)
+            keep2[k] = jnp.where(y0 == 0, total[0], total[1])
+            out2[k] = jnp.where(y0 == 0, total[1], total[0]).astype(jnp.bfloat16)
+            row_copy(k).start()
+
+        @pl.when((i >= 3) & (i < o_chunks + 3))
+        def _():
+            k = i - 3
+            row_copy(k).wait_recv()
+            total = keep2[k] + in2[k].astype(jnp.float32)
+            total = total.reshape(at_count, tok_rows, O_COLS)
+            out3[k] = total.astype(jnp.bfloat16)
+            which = lax.broadcasted_iota(jnp.int32, total.shape, 0)
+            keep3[k] = jnp.sum(jnp.where(which == a0, total, 0.0), axis=0)
+            for j in range(1, at_count):
+                col_copy(k, j).start()
+
+        @pl.when(i >= 5)
+        def _():
+            k = i - 5
+            for j in range(1, at_count):
+                col_copy(k, j).wait_recv()
+            total = keep3[k] + jnp.sum(in3[k].astype(jnp.float32), axis=0)
+            o_ref[:, pl.ds(pl.multiple_of(k * O_COLS, O_COLS), O_COLS)] = total.astype(jnp.bfloat16)
+            core_copy(k).wait_send()
+            row_copy(k).wait_send()
+            for j in range(1, at_count):
+                col_copy(k, j).wait_send()
+
+        return carry
+
+    lax.fori_loop(0, o_chunks + 5, down, 0)
+    for j in range(1, at_count):
+        z_copy(j, own).wait_send()
+    for j in range(at_count):
+        y_copy(j, block(e0, j)).wait_send()
+        c_copy(j, block(e0, j)).wait_send()
+        c_copy(4 + j, block(e_y, j)).wait_send()
+
+
+def fused_experts(tokens, expert_ids, gates, w_in, w_out):
+    tok_rows, model_width = tokens.shape
+    slot_count, _, pair, hid_units = w_in.shape
+    rows = 16 * tok_rows
+    chunks = model_width // O_COLS
+    jbs = hid_units // LANES
+    hit = expert_ids[:, :, None] == jnp.arange(LANES)[None, None, :]
+    dense = jnp.sum(jnp.where(hit, gates[:, :, None], jnp.bfloat16(0)), axis=1)
+    block = jnp.concatenate([tokens, dense.astype(jnp.bfloat16)], axis=1)
+    view = w_in.reshape(slot_count, model_width, pair, jbs, LANES).transpose(0, 1, 3, 2, 4)
+    bf16, f32 = jnp.bfloat16, jnp.float32
+    dma = pltpu.SemaphoreType.DMA
+    return pl.pallas_call(
+        moe_kernel,
+        out_shape=jax.ShapeDtypeStruct((tok_rows, model_width), bf16),
+        in_specs=[
+            pl.BlockSpec(memory_space=pltpu.VMEM),
+            pl.BlockSpec(memory_space=pl.ANY),
+            pl.BlockSpec(memory_space=pl.ANY),
+        ],
+        out_specs=pl.BlockSpec(memory_space=pltpu.VMEM),
+        scratch_shapes=[
+            pltpu.VMEM((16, tok_rows, model_width + LANES), bf16),
+            pltpu.VMEM((2 * rows, 2 * model_width), bf16),
+            pltpu.VMEM((W_SLOTS, jbs, D_BLOCK, 2, LANES), bf16),
+            pltpu.VMEM((O_SLOTS, slot_count, hid_units, O_COLS), bf16),
+            pltpu.VMEM((2 * rows, hid_units), f32),
+            pltpu.VMEM((rows, slot_count * hid_units), bf16),
+            pltpu.VMEM((chunks, 2, rows // 4, O_COLS), f32),
+            pltpu.VMEM((chunks, 2, rows // 4, O_COLS), bf16),
+            pltpu.VMEM((chunks, 2, rows // 4, O_COLS), bf16),
+            pltpu.VMEM((chunks, rows // 4, O_COLS), f32),
+            pltpu.VMEM((chunks, rows // 4, O_COLS), bf16),
+            pltpu.VMEM((chunks, rows // 4, O_COLS), bf16),
+            pltpu.VMEM((chunks, tok_rows, O_COLS), f32),
+            pltpu.VMEM((chunks, 4, tok_rows, O_COLS), bf16),
+            pltpu.VMEM((chunks, 3, tok_rows, O_COLS), bf16),
+            dma((W_SLOTS, jbs)), dma((O_SLOTS,)),
+            dma((3,)), dma((3,)), dma((4,)), dma((4,)), dma((8,)), dma((8,)),
+            dma((chunks,)), dma((chunks,)), dma((chunks,)), dma((chunks,)),
+            dma((chunks, 3)), dma((chunks, 3)),
+        ],
+        compiler_params=pltpu.CompilerParams(
+            collective_id=0, has_side_effects=True, vmem_limit_bytes=61 << 20
+        ),
+    )(block, view, w_out)
 
 
 def expert_part(row_block, row_gates, w_in, w_out):
@@ -37,8 +297,8 @@
     return context.astype(jnp.bfloat16)
 
 
-def per_device(
-    tokens, expert_ids, gates, w_in, w_out, q_latent, q_rope, cache_latent, cache_rope, lengths
+def routed_experts(
+    tokens, expert_ids, gates, w_in, w_out
 ):
     tok_rows, model_width = tokens.shape
     top_count = expert_ids.shape[1]
@@ -86,13 +346,22 @@
     )
     flat_out = out_rows.reshape(slot_rows, model_width)
     moe_out = jnp.sum(flat_out[target.reshape(tok_rows, top_count)], axis=1).astype(jnp.bfloat16)
+    return moe_out
+
+
+def per_device(
+    fused, tokens, expert_ids, gates, w_in, w_out, q_latent, q_rope, cache_latent, cache_rope, lengths
+):
+    layer = fused_experts if fused else routed_experts
+    moe_out = layer(tokens, expert_ids, gates, w_in, w_out)
     context = latent_attention(q_latent, q_rope, cache_latent, cache_rope, lengths)
     return (moe_out, context)
 
 
 def solution(mesh):
+    fused = mesh.shape["ex"] == 4 and mesh.shape["at"] == 4
     return jax.shard_map(
-        per_device,
+        functools.partial(per_device, fused),
         mesh=mesh,
         in_specs=(
             P(("grp", "ex", "at"), None),

time: 304 us -> 106 us (0.35)
  local copies, waits for them, and re-layouts: 120 us -> 2.86 us
  waiting for transfers between devices: 110 us -> 0 us
  Pallas kernels: 0 us -> 94.7 us
  matrix products: 43.3 us -> 3.73 us
  starting transfers between devices: 18.4 us -> 0 us
  other arithmetic: 9.11 us -> 3.36 us
    all_to_all x3 -> x0, waiting for transfers between devices: 110 us -> none  [the longest x1 100 us: per_device(): lax.all_to_all(partial_value, ('ex', 'at'), split_axis=1, concat_axis=1,...]
    reshape x3 -> x0, local copies, waits for them, and re-layouts: 95.9 us -> none  [the longest x1 92.8 us: expert_part(): w_in.reshape(slot_count, model_width, pair_count * hid_units)]
    pallas_call x0 -> x1, Pallas kernels: none -> 94.7 us  [fused_experts(): pl.pallas_call(moe_kernel, out_shape=jax.ShapeDtypeStruct((tok_rows, mode...]
    dot_general x4 -> x0, matrix products: 41.4 us -> none  [the longest x1 22.2 us: expert_part(): jnp.einsum('srd,sdf->srf', row_block, w_in.reshape(slot_count, model_widt...]
    all_to_all x3 -> x0, starting transfers between devices: 18.4 us -> none  [the longest x1 7.39 us: per_device(): lax.all_to_all(spread_gates, ('ex', 'at'), split_axis=1, concat_axis=1, t...]
    broadcast_in_dim x7 -> x0, local copies, waits for them, and re-layouts: 9.15 us -> none  [the longest x3 8.34 us: per_device(): jnp.broadcast_to(packed[:, :, None], (slot_count, ex_count, at_count, CAP...]
    convert_element_type x3 -> x0, local copies, waits for them, and re-layouts: 8.09 us -> none  [the longest x1 7.89 us: expert_part(): (down_out * row_gates[..., None].astype(jnp.float32)).astype(jnp.bfloat16)]
    reduce_sum x3 -> x1, other arithmetic: 7.84 us -> 0.79 us  [fused_experts(): dense = jnp.sum(jnp.where(hit, gates[:, :, None], jnp.bfloat16(0)), axis=1)]
  transfers between devices with their start and end apart: 3 -> 0, of which waited for: 2 -> 0; matrix products, arithmetic and copies ran while one was open for 34% -> 0% of each run, Pallas kernels for 0% -> 0%
where the time goes in v1:
time: 106 us; the launch traced here: 105 us
  Pallas kernels  94.7 us (89%)
  matrix products  3.73 us (4%)
  other arithmetic  3.36 us (3%)
  local copies, waits for them, and re-layouts  2.86 us (3%)
    pallas_call x1, Pallas kernels, fused_experts(): pl.pallas_call(moe_kernel, out_shape=jax.ShapeDtypeStruct((tok_rows, mode...  94.7 us

profile of v1, /device:TPU:0, one launch (start us, length us, event | category | flops | bytes accessed | tf_op | source)
XLA Modules:
  0.0 105.3 jit_solution(10936694553135507300)
XLA Ops:
  0.6 0.0 copy-start
  0.6 0.8 iota_compare_fusion.1
  1.5 0.4 copy-done
  1.9 1.4 %fusion.12 = f32[4,64,256]{2,1,0:T(8,128)S(1)} fusion(bf16[4,64,512]{2,1,0:T(8,128)(2,1)} %param.15, bf16[4,256,512]{2,1,0:T(8,128)(2,1)S(1)} %copy-done), kind=kOutput, calls=%fused_computation.18 | convolution fusion | flops 67108864 | bytes 1572864 | tf_op jit(solution)/shard_map/ahl,acl->ahc/dot_general | solution.py:286
  3.3 0.9 reshape.36
  4.1 1.1 %fusion.3 = f32[4,64,256]{2,1,0:T(8,128)S(1)} fusion(f32[4,64,256]{2,1,0:T(8,128)S(1)} %fusion.12, bf16[4,64,64]{2,1,0:T(8,128)(2,1)S(1)} %reshape.36, bf16[4,64,256]{2,1,0:T(8,128)(2,1)} %param.18, pred[4,256]{1,0:T(4,128)(4,1)S(1)} %iota_compare_fusion.1), kind=kOutput, calls=%fused_computation.5 | convolution fusion | flops 8585216 | bytes 689152 | tf_op jit(solution)/shard_map/ahr,arc->ahc/dot_general | solution.py:287
  5.2 0.2 fusion.11
  5.4 1.3 %convolution_convert_fusion = bf16[4,64,512]{2,1,0:T(8,128)(2,1)} fusion(bf16[4,256,512]{2,1,0:T(8,128)(2,1)S(1)} %copy-done, f32[4,64]{1,0:T(4,128)S(1)} %fusion.11, f32[4,64,256]{2,1,0:T(8,128)S(1)} %fusion.3, pred[4,256]{1,0:T(4,128)(4,1)S(1)} %iota_compare_fusion.1), kind=kOutput, calls=%fused_computation.2 | convolution fusion | flops 67502592 | bytes 1574912 | tf_op jit(solution)/shard_map/ahc,acl->ahl/dot_general | solution.py:296
  6.7 0.8 fusion.8
  7.5 1.5 %pad_maximum_fusion.x_ref = bf16[8,7296]{1,0:T(8,128)(2,1)} fusion(bf16[8,128]{1,0:T(8,128)(2,1)S(1)} %fusion.8, bf16[8,7168]{1,0:T(8,128)(2,1)} %param.10), kind=kLoop, calls=%fused_computation.10 | loop fusion | flops 233472 | bytes 233472 | tf_op jit(solution)/shard_map/concatenate | solution.py:229
  9.1 94.7 %shard_map.113 = bf16[8,7168]{1,0:T(8,128)(2,1)} custom-call(bf16[8,7296]{1,0:T(8,128)(2,1)} %pad_maximum_fusion.x_ref, bf16[4,7168,4,2,128]{4,3,2,1,0:T(2,128)(2,1)} %bitcast.10, bf16[4,512,7168]{2,1,0:T(8,128)(2,1)} %wout_ref.1), custom_call_target="tpu_custom_call" | custom-call | tf_op jit(solution)/shard_map/pallas_call | solution.py:233
  103.8 1.6 %copy.13 = bf16[8,7168]{1,0:T(8,128)(2,1)} copy(bf16[8,7168]{1,0:T(8,128)(2,1)} %shard_map.113) | data formatting | bytes 229376
Async XLA Ops:
  0.6 1.2 %copy-start = (bf16[4,256,512]{2,1,0:T(8,128)(2,1)S(1)}, bf16[4,256,512]{2,1,0:T(8,128)(2,1)}, u32[]{:S(2)}) copy-start(bf16[4,256,512]{2,1,0:T(8,128)(2,1)} %param.17) | copy-start | bytes 3145732

commit v2 on v1

--- a/solution.py
+++ b/solution.py
@@ -10,18 +10,19 @@
 CAP = 5
 LANES = 128
 D_BLOCK = 1024
-W_SLOTS = 12
+W_SLOTS = 11
 O_COLS = 512
 O_SLOTS = 6
 
 
 def moe_kernel(
-    x_ref, win_ref, wout_ref, o_ref,
+    x_ref, win_ref, wout_ref, ql_ref, qr_ref, cl_ref, cp_ref, len_ref, o_ref, ctx_ref,
     xg, xe, wbuf, obuf, acc, hid, keep1, out1, in1, keep2, out2, in2, keep3, out3, in3,
     wsem, osem, zs, zr, ys, yr, cs, cr, s1, q1, s2, q2, s3, q3,
 ):
-    experts_here, model_width, jbs = win_ref.shape[:3]
-    hid_units = wout_ref.shape[1]
+    experts_here, model_width, pair, hid_units = win_ref.shape
+    jbs = hid_units // LANES
+    win_rows = win_ref.reshape(experts_here, model_width * pair, hid_units)
     at_count = 4
     tok_rows = x_ref.shape[0]
     rows = 16 * tok_rows
@@ -37,7 +38,11 @@
 
     def w_copy(i, jb):
         return pltpu.make_async_copy(
-            win_ref.at[i // d_chunks, pl.ds((i % d_chunks) * D_BLOCK, D_BLOCK), jb],
+            win_rows.at[
+                i // d_chunks,
+                pl.ds(pl.multiple_of((i % d_chunks) * 2 * D_BLOCK, 2 * D_BLOCK), 2 * D_BLOCK),
+                pl.ds(jb * LANES, LANES),
+            ],
             wbuf.at[i % W_SLOTS, jb],
             wsem.at[i % W_SLOTS, jb],
         )
@@ -93,10 +98,29 @@
     y_copy(0, own).start()
     c_copy(0, own).start()
     lax.fori_loop(0, O_SLOTS, o_start, 0)
+    def attend(r):
+        last = (((1,), (1,)), ((), ()))
+        latent = cl_ref[r]
+        scores = lax.dot_general(ql_ref[r], latent, last, preferred_element_type=jnp.float32)
+        scores = scores + jnp.dot(qr_ref[r], cp_ref[r], preferred_element_type=jnp.float32)
+        scores = scores * 192.0 ** (-0.5)
+        visible = lax.broadcasted_iota(jnp.int32, scores.shape, 1) < len_ref[r]
+        scores = jnp.where(visible, scores, -1e30)
+        peak = jnp.max(scores, axis=1, keepdims=True)
+        expo = jnp.where(visible, jnp.exp(scores - peak), 0.0)
+        probs = (expo / jnp.sum(expo, axis=1, keepdims=True)).astype(jnp.bfloat16)
+        context = jnp.dot(probs, latent, preferred_element_type=jnp.float32)
+        ctx_ref[r] = context.astype(jnp.bfloat16)
+
+    att_rows = ql_ref.shape[0]
     for j in (1, 3, 2):
+        if j - 1 < att_rows:
+            attend(j - 1)
         z_copy(j, block(e0, j)).wait_recv()
         y_copy(j, block(e0, j)).start()
         c_copy(j, block(e0, j)).start()
+    for r in range(3, att_rows):
+        attend(r)
     for j in (0, 1, 3, 2):
         y_copy(j, block(e_y, j)).wait_recv()
         c_copy(4 + j, block(e_y, j)).start()
@@ -129,9 +153,8 @@
             i = e * d_chunks + d
             for jb in range(jbs):
                 w_copy(i, jb).wait()
-            view = wbuf.at[i % W_SLOTS].reshape(jbs, 2 * D_BLOCK, LANES)
             x = xe[:, pl.ds(pl.multiple_of(d * 2 * D_BLOCK, 2 * D_BLOCK), 2 * D_BLOCK)]
-            w = jnp.concatenate([view[jb] for jb in range(jbs)], axis=1)
+            w = jnp.concatenate([wbuf[i % W_SLOTS, jb] for jb in range(jbs)], axis=1)
             acc[...] += jnp.dot(x, w, preferred_element_type=jnp.float32)
 
             @pl.when(i + W_SLOTS < w_chunks)
@@ -218,31 +241,44 @@
         c_copy(4 + j, block(e_y, j)).wait_send()
 
 
-def fused_experts(tokens, expert_ids, gates, w_in, w_out):
+def fused_layers(
+    tokens, expert_ids, gates, w_in, w_out, q_latent, q_rope, cache_latent, cache_rope, lengths
+):
     tok_rows, model_width = tokens.shape
-    slot_count, _, pair, hid_units = w_in.shape
+    slot_count, _, _, hid_units = w_in.shape
     rows = 16 * tok_rows
     chunks = model_width // O_COLS
     jbs = hid_units // LANES
     hit = expert_ids[:, :, None] == jnp.arange(LANES)[None, None, :]
     dense = jnp.sum(jnp.where(hit, gates[:, :, None], jnp.bfloat16(0)), axis=1)
     block = jnp.concatenate([tokens, dense.astype(jnp.bfloat16)], axis=1)
-    view = w_in.reshape(slot_count, model_width, pair, jbs, LANES).transpose(0, 1, 3, 2, 4)
+    rope_q = q_rope.reshape(q_latent.shape[0], q_latent.shape[1], -1)
     bf16, f32 = jnp.bfloat16, jnp.float32
     dma = pltpu.SemaphoreType.DMA
     return pl.pallas_call(
         moe_kernel,
-        out_shape=jax.ShapeDtypeStruct((tok_rows, model_width), bf16),
+        out_shape=(
+            jax.ShapeDtypeStruct((tok_rows, model_width), bf16),
+            jax.ShapeDtypeStruct(q_latent.shape, bf16),
+        ),
         in_specs=[
             pl.BlockSpec(memory_space=pltpu.VMEM),
             pl.BlockSpec(memory_space=pl.ANY),
             pl.BlockSpec(memory_space=pl.ANY),
+            pl.BlockSpec(memory_space=pltpu.VMEM),
+            pl.BlockSpec(memory_space=pltpu.VMEM),
+            pl.BlockSpec(memory_space=pltpu.VMEM),
+            pl.BlockSpec(memory_space=pltpu.VMEM),
+            pl.BlockSpec(memory_space=pltpu.SMEM),
         ],
-        out_specs=pl.BlockSpec(memory_space=pltpu.VMEM),
+        out_specs=(
+            pl.BlockSpec(memory_space=pltpu.VMEM),
+            pl.BlockSpec(memory_space=pltpu.VMEM),
+        ),
         scratch_shapes=[
             pltpu.VMEM((16, tok_rows, model_width + LANES), bf16),
             pltpu.VMEM((2 * rows, 2 * model_width), bf16),
-            pltpu.VMEM((W_SLOTS, jbs, D_BLOCK, 2, LANES), bf16),
+            pltpu.VMEM((W_SLOTS, jbs, 2 * D_BLOCK, LANES), bf16),
             pltpu.VMEM((O_SLOTS, slot_count, hid_units, O_COLS), bf16),
             pltpu.VMEM((2 * rows, hid_units), f32),
             pltpu.VMEM((rows, slot_count * hid_units), bf16),
@@ -263,7 +299,7 @@
         compiler_params=pltpu.CompilerParams(
             collective_id=0, has_side_effects=True, vmem_limit_bytes=61 << 20
         ),
-    )(block, view, w_out)
+    )(block, w_in, w_out, q_latent, rope_q, cache_latent, cache_rope, lengths)
 
 
 def expert_part(row_block, row_gates, w_in, w_out):
@@ -352,8 +388,11 @@
 def per_device(
     fused, tokens, expert_ids, gates, w_in, w_out, q_latent, q_rope, cache_latent, cache_rope, lengths
 ):
-    layer = fused_experts if fused else routed_experts
-    moe_out = layer(tokens, expert_ids, gates, w_in, w_out)
+    if fused:
+        return fused_layers(
+            tokens, expert_ids, gates, w_in, w_out, q_latent, q_rope, cache_latent, cache_rope, lengths
+        )
+    moe_out = routed_experts(tokens, expert_ids, gates, w_in, w_out)
     context = latent_attention(q_latent, q_rope, cache_latent, cache_rope, lengths)
     return (moe_out, context)
 

time: 106 us -> 91.2 us (0.86)
  Pallas kernels: 94.7 us -> 83.2 us
  matrix products: 3.73 us -> 0 us
  local copies, waits for them, and re-layouts: 2.86 us -> 4.73 us
    pallas_call x1, Pallas kernels: 94.7 us -> 83.2 us  [fused_layers(): pl.pallas_call(moe_kernel, out_shape=(jax.ShapeDtypeStruct((tok_rows, mod...]
    dot_general x3 -> x0, matrix products: 3.73 us -> none  [the longest x1 1.38 us: latent_attention(): jnp.einsum('ahl,acl->ahc', q_latent, cache_latent, preferred_element_type...]
    unnamed x3 -> x2, local copies, waits for them, and re-layouts: 1.98 us -> 3.22 us
where the time goes in v2:
time: 91.2 us; the launch traced here: 90.9 us
  Pallas kernels  83.2 us (91%)
  local copies, waits for them, and re-layouts  4.73 us (5%)
  other arithmetic  2.34 us (3%)
    pallas_call x1, Pallas kernels, fused_layers(): pl.pallas_call(moe_kernel, out_shape=(jax.ShapeDtypeStruct((tok_rows, mod...  83.2 us
    unnamed x2, local copies, waits for them, and re-layouts  3.22 us

profile of v2, /device:TPU:0, one launch (start us, length us, event | category | flops | bytes accessed | tf_op | source)
XLA Modules:
  0.0 90.9 jit_solution(2675377534400497705)
XLA Ops:
  0.6 0.8 fusion.1
  1.4 1.5 %reshape.9.qr_ref = bf16[4,64,64]{2,1,0:T(8,128)(2,1)} reshape(bf16[4,4096]{1,0:T(4,128)(2,1)} %param.16) | data formatting | bytes 65536 | tf_op jit(solution)/shard_map/reshape | solution.py:255
  2.9 1.6 %pad_maximum_fusion.x_ref = bf16[8,7296]{1,0:T(8,128)(2,1)} fusion(bf16[8,128]{1,0:T(8,128)(2,1)S(1)} %fusion.1, bf16[8,7168]{1,0:T(8,128)(2,1)} %param.10), kind=kLoop, calls=%fused_computation | loop fusion | flops 233472 | bytes 233472 | tf_op jit(solution)/shard_map/concatenate | solution.py:254
  4.5 83.2 %shard_map.113 = (bf16[8,7168]{1,0:T(8,128)(2,1)}, bf16[4,64,512]{2,1,0:T(8,128)(2,1)}) custom-call(bf16[8,7296]{1,0:T(8,128)(2,1)} %pad_maximum_fusion.x_ref, bf16[4,7168,2,512]{3,2,1,0:T(2,128)(2,1)} %win_ref.1, bf16[4,512,7168]{2,1,0:T(8,128)(2,1)} %wout_ref.1, bf16[4,64,512]{2,1,0:T(8,128)(2,1)} %ql_ref.1, bf16[4,64,64]{2,1,0:T(8,128)(2,1)} %reshape.9.qr_ref, ...), custom_call_target="tpu_custom_call" | custom-call | tf_op jit(solution)/shard_map/pallas_call | solution.py:258
  87.7 1.6 %copy.14 = bf16[8,7168]{1,0:T(8,128)(2,1)} copy(bf16[8,7168]{1,0:T(8,128)(2,1)} %get-tuple-element.4) | data formatting | bytes 229376
  89.2 1.7 %copy.15 = bf16[4,64,512]{2,1,0:T(8,128)(2,1)} copy(bf16[4,64,512]{2,1,0:T(8,128)(2,1)} %get-tuple-element.5) | data formatting | bytes 524288

commit v3 on v2

--- a/solution.py
+++ b/solution.py
@@ -133,16 +133,21 @@
     col = lax.broadcasted_iota(jnp.int32, (LANES, 2 * LANES), 1)
     spread = [(col == 2 * row + p).astype(jnp.bfloat16) for p in range(2)]
 
-    def expand(i, carry):
-        x = xg[:, :, pl.ds(pl.multiple_of(i * LANES, LANES), LANES)].astype(jnp.float32)
-        x = x.reshape(rows, LANES).astype(jnp.bfloat16)
-        for p in range(2):
-            xe[p * rows:(p + 1) * rows, pl.ds(pl.multiple_of(i * 2 * LANES, 2 * LANES), 2 * LANES)] = (
-                jnp.dot(x, spread[p], preferred_element_type=jnp.float32).astype(jnp.bfloat16)
-            )
+    group = 8
+
+    def expand(g, carry):
+        for u in range(group):
+            i = g * group + u
+            x = xg[:, :, pl.ds(pl.multiple_of(i * LANES, LANES), LANES)].astype(jnp.float32)
+            x = x.reshape(rows, LANES).astype(jnp.bfloat16)
+            wide = pl.ds(pl.multiple_of(i * 2 * LANES, 2 * LANES), 2 * LANES)
+            for p in range(2):
+                xe[p * rows:(p + 1) * rows, wide] = jnp.dot(
+                    x, spread[p], preferred_element_type=jnp.float32
+                ).astype(jnp.bfloat16)
         return carry
 
-    lax.fori_loop(0, model_width // LANES, expand, 0)
+    lax.fori_loop(0, model_width // (LANES * group), expand, 0)
     dense = xg[:, :, model_width:model_width + LANES].astype(jnp.float32).reshape(rows, LANES)
     lane = lax.broadcasted_iota(jnp.int32, (rows, LANES), 1)
 

time: 91.2 us -> 84.4 us (0.925)
  Pallas kernels: 83.2 us -> 76.3 us
    pallas_call x1, Pallas kernels: 83.2 us -> 76.3 us  [fused_layers(): pl.pallas_call(moe_kernel, out_shape=(jax.ShapeDtypeStruct((tok_rows, mod...]
where the time goes in v3:
time: 84.4 us; the launch traced here: 84 us
  Pallas kernels  76.3 us (90%)
  local copies, waits for them, and re-layouts  4.73 us (6%)
  other arithmetic  2.34 us (3%)
    pallas_call x1, Pallas kernels, fused_layers(): pl.pallas_call(moe_kernel, out_shape=(jax.ShapeDtypeStruct((tok_rows, mod...  76.3 us
    unnamed x2, local copies, waits for them, and re-layouts  3.22 us

profile of v3, /device:TPU:0, one launch (start us, length us, event | category | flops | bytes accessed | tf_op | source)
XLA Modules:
  0.0 84.0 jit_solution(11284143311478242175)
XLA Ops:
  0.6 0.8 fusion.1
  1.4 1.5 %reshape.9.qr_ref = bf16[4,64,64]{2,1,0:T(8,128)(2,1)} reshape(bf16[4,4096]{1,0:T(4,128)(2,1)} %param.16) | data formatting | bytes 65536 | tf_op jit(solution)/shard_map/reshape | solution.py:260
  2.9 1.6 %pad_maximum_fusion.x_ref = bf16[8,7296]{1,0:T(8,128)(2,1)} fusion(bf16[8,128]{1,0:T(8,128)(2,1)S(1)} %fusion.1, bf16[8,7168]{1,0:T(8,128)(2,1)} %param.10), kind=kLoop, calls=%fused_computation | loop fusion | flops 233472 | bytes 233472 | tf_op jit(solution)/shard_map/concatenate | solution.py:259
  4.5 76.3 %shard_map.113 = (bf16[8,7168]{1,0:T(8,128)(2,1)}, bf16[4,64,512]{2,1,0:T(8,128)(2,1)}) custom-call(bf16[8,7296]{1,0:T(8,128)(2,1)} %pad_maximum_fusion.x_ref, bf16[4,7168,2,512]{3,2,1,0:T(2,128)(2,1)} %win_ref.1, bf16[4,512,7168]{2,1,0:T(8,128)(2,1)} %wout_ref.1, bf16[4,64,512]{2,1,0:T(8,128)(2,1)} %ql_ref.1, bf16[4,64,64]{2,1,0:T(8,128)(2,1)} %reshape.9.qr_ref, ...), custom_call_target="tpu_custom_call" | custom-call | tf_op jit(solution)/shard_map/pallas_call | solution.py:263
  80.8 1.6 %copy.14 = bf16[8,7168]{1,0:T(8,128)(2,1)} copy(bf16[8,7168]{1,0:T(8,128)(2,1)} %get-tuple-element.4) | data formatting | bytes 229376
  82.4 1.7 %copy.15 = bf16[4,64,512]{2,1,0:T(8,128)(2,1)} copy(bf16[4,64,512]{2,1,0:T(8,128)(2,1)} %get-tuple-element.5) | data formatting | bytes 524288

commit v4 on v3

--- a/solution.py
+++ b/solution.py
@@ -202,18 +202,18 @@
             def _():
                 o_start(i + O_SLOTS, 0)
 
-        @pl.when((i >= 1) & (i < o_chunks + 1))
+        @pl.when((i >= 2) & (i < o_chunks + 2))
         def _():
-            k = i - 1
+            k = i - 2
             core_copy(k).wait_recv()
             total = keep1[k] + in1[k].astype(jnp.float32)
             keep2[k] = jnp.where(y0 == 0, total[0], total[1])
             out2[k] = jnp.where(y0 == 0, total[1], total[0]).astype(jnp.bfloat16)
             row_copy(k).start()
 
-        @pl.when((i >= 3) & (i < o_chunks + 3))
+        @pl.when((i >= 6) & (i < o_chunks + 6))
         def _():
-            k = i - 3
+            k = i - 6
             row_copy(k).wait_recv()
             total = keep2[k] + in2[k].astype(jnp.float32)
             total = total.reshape(at_count, tok_rows, O_COLS)
@@ -223,9 +223,9 @@
             for j in range(1, at_count):
                 col_copy(k, j).start()
 
-        @pl.when(i >= 5)
+        @pl.when(i >= 9)
         def _():
-            k = i - 5
+            k = i - 9
             for j in range(1, at_count):
                 col_copy(k, j).wait_recv()
             total = keep3[k] + jnp.sum(in3[k].astype(jnp.float32), axis=0)
@@ -237,7 +237,7 @@
 
         return carry
 
-    lax.fori_loop(0, o_chunks + 5, down, 0)
+    lax.fori_loop(0, o_chunks + 9, down, 0)
     for j in range(1, at_count):
         z_copy(j, own).wait_send()
     for j in range(at_count):

time: 84.4 us -> 79.2 us (0.938)
  Pallas kernels: 76.3 us -> 71.2 us
    pallas_call x1, Pallas kernels: 76.3 us -> 71.2 us  [fused_layers(): pl.pallas_call(moe_kernel, out_shape=(jax.ShapeDtypeStruct((tok_rows, mod...]
where the time goes in v4:
time: 79.2 us; the launch traced here: 78.9 us
  Pallas kernels  71.2 us (90%)
  local copies, waits for them, and re-layouts  4.73 us (6%)
  other arithmetic  2.34 us (3%)
    pallas_call x1, Pallas kernels, fused_layers(): pl.pallas_call(moe_kernel, out_shape=(jax.ShapeDtypeStruct((tok_rows, mod...  71.2 us
    unnamed x2, local copies, waits for them, and re-layouts  3.22 us

profile of v4, /device:TPU:0, one launch (start us, length us, event | category | flops | bytes accessed | tf_op | source)
XLA Modules:
  0.0 78.9 jit_solution(12591423756578285307)
XLA Ops:
  0.6 0.8 %fusion.1 = bf16[8,128]{1,0:T(8,128)(2,1)S(1)} fusion(s32[8,8]{1,0:T(8,128)} %param.11, bf16[8,8]{1,0:T(8,128)(2,1)} %param.12), kind=kLoop, calls=%fused_computation.3 | loop fusion | flops 23552 | bytes 2432 | tf_op jit(solution)/shard_map/reduce_sum | solution.py:258
  1.4 1.5 %reshape.9.qr_ref = bf16[4,64,64]{2,1,0:T(8,128)(2,1)} reshape(bf16[4,4096]{1,0:T(4,128)(2,1)} %param.16) | data formatting | bytes 65536 | tf_op jit(solution)/shard_map/reshape | solution.py:260
  2.9 1.6 %pad_maximum_fusion.x_ref = bf16[8,7296]{1,0:T(8,128)(2,1)} fusion(bf16[8,128]{1,0:T(8,128)(2,1)S(1)} %fusion.1, bf16[8,7168]{1,0:T(8,128)(2,1)} %param.10), kind=kLoop, calls=%fused_computation | loop fusion | flops 233472 | bytes 233472 | tf_op jit(solution)/shard_map/concatenate | solution.py:259
  4.5 71.2 %shard_map.113 = (bf16[8,7168]{1,0:T(8,128)(2,1)}, bf16[4,64,512]{2,1,0:T(8,128)(2,1)}) custom-call(bf16[8,7296]{1,0:T(8,128)(2,1)} %pad_maximum_fusion.x_ref, bf16[4,7168,2,512]{3,2,1,0:T(2,128)(2,1)} %win_ref.1, bf16[4,512,7168]{2,1,0:T(8,128)(2,1)} %wout_ref.1, bf16[4,64,512]{2,1,0:T(8,128)(2,1)} %ql_ref.1, bf16[4,64,64]{2,1,0:T(8,128)(2,1)} %reshape.9.qr_ref, ...), custom_call_target="tpu_custom_call" | custom-call | tf_op jit(solution)/shard_map/pallas_call | solution.py:263
  75.7 1.6 %copy.14 = bf16[8,7168]{1,0:T(8,128)(2,1)} copy(bf16[8,7168]{1,0:T(8,128)(2,1)} %get-tuple-element.4) | data formatting | bytes 229376
  77.3 1.7 %copy.15 = bf16[4,64,512]{2,1,0:T(8,128)(2,1)} copy(bf16[4,64,512]{2,1,0:T(8,128)(2,1)} %get-tuple-element.5) | data formatting | bytes 524288
